TPU v7x, 32 devices: a whole 2x2x4 slice. The times are simulated.
32 devices in a mesh: dp: 8 (over z, x), mp: 4 (over y, core).
Axes of the slice: x: 2, y: 2, z: 4, core: 2. Of those that a mesh axis runs over, the one named last changes fastest.
Arguments:
- hidden: bfloat16 [10240, 8192], P('dp', 'mp'), may hold values from -6 to 6
- rewards: float32 [64, 160], P('dp'), may hold values from -4 to 4
- lengths: int32 [64], P('dp'), may hold values from 1 to 160, as said below
- dest_shard: int32 [64], P('dp'), may hold values from 0 to 7, as said below
- source_owner: int32 [64], P('dp'), may hold values from 0 to 7, as said below
- pack_offset: int32 [64], P('dp'), may hold values from 0 to 639, as said below
- segment_ids: int32 [5120], P('dp'), may hold values from 0 to 7, as said below
- norm_gain: float32 [8192], replicated, may hold values from 0.5 to 1.5
- w_query: bfloat16 [8192, 4096], P(None, 'mp'), may hold values from -1 to 1
- w_key: bfloat16 [8192, 512], P(None, 'mp'), may hold values from -1 to 1
- w_value: bfloat16 [8192, 512], P(None, 'mp'), may hold values from -0.0625 to 0.0625
- value_head: float32 [8192], P('mp'), may hold values from -0.0625 to 0.0625
- folded_head: float32 [4096], P('mp'), may hold values from -0.09375 to 0.09375
Outputs:
- values: float32 [64, 160], P('dp')
- advantages: float32 [64, 160], P('dp')
Inputs may be any that keep to these rules, and one draw needn't show every extreme that they name: `lengths`: rows of a slot past its rollout's length are unused. Every critic shard holds a rollout of 160 rows. Some owner's 8 rollouts all have 160 rows. `dest_shard`: owner o packs its 8 rollouts on the shards o, o + 1, ..., o + 7, modulo the number of shards, one on each. `source_owner`: shard s packs one rollout from each of the owners s, s - 1, ..., s - 7, modulo the number of shards, in some order, agreeing with dest_shard. `pack_offset`: A shard's packed rollouts lie back to back in the order of their index, each with the length that lengths gives it, and fill all 640 rows. `segment_ids`: each packed row names the index of the packed rollout that holds it, as pack_offset and lengths lay them out.
All inputs are finite; a program needn't handle non-finite values.
Results may differ from a plain program's by a relative error of at most 0.007.
Values may be sent and summed in bfloat16 or wider, within the bound.
No kernel may reach another device: no remote copies, remote signals or barrier semaphores. Data moves between devices by JAX's collectives and lax.ppermute only.
A program may use at most 192 MiB of HBM per device.

v0:
```python
import math

import jax
import jax.numpy as jnp
from jax import lax
from jax.sharding import PartitionSpec as P

HD = 128


EPSILON = 1e-05
DISCOUNT = 0.99
SMOOTHING = 0.95
ROPE_BASE = 500000.0


def passed_along(value, axis, by):
    length = lax.axis_size(axis)
    return lax.ppermute(value, axis, [(i, (i + by) % length) for i in range(length)])


def rotary(values_in, positions):
    half_width = values_in.shape[-1] // 2
    frequency = ROPE_BASE ** (-jnp.arange(half_width, dtype=jnp.float32) / half_width)
    angles = positions.astype(jnp.float32)[:, None] * frequency[None, :]
    cosine = jnp.cos(angles)[:, None, :]
    sine_part = jnp.sin(angles)[:, None, :]
    front_half = values_in[..., :half_width]
    back_half = values_in[..., half_width:]
    return jnp.concatenate(
        [front_half * cosine - back_half * sine_part, back_half * cosine + front_half * sine_part],
        axis=-1,
    )


def head_values(queries, keys_out, values_out, segments, positions, folded_head):
    row_count = queries.shape[0]
    kv_count = keys_out.shape[1] // HD
    group_size = queries.shape[1] // HD // kv_count
    query_rot = rotary(queries.reshape(row_count, kv_count * group_size, HD), positions).astype(
        jnp.bfloat16
    )
    query_rot = query_rot.reshape(row_count, kv_count, group_size, HD)
    key_rot = rotary(keys_out.reshape(row_count, kv_count, HD), positions).astype(jnp.bfloat16)
    value_rows = values_out.astype(jnp.bfloat16).reshape(row_count, kv_count, HD)
    scores = jnp.einsum(
        "qhgd,khd->hgqk", query_rot, key_rot, preferred_element_type=jnp.float32
    ) / math.sqrt(HD)
    allowed = (segments[:, None] == segments[None, :]) & (positions[:, None] >= positions[None, :])
    scores = jnp.where(allowed[None, None], scores, -1e30)
    row_max = jnp.max(scores, axis=-1, keepdims=True)
    exp_scores = jnp.where(allowed[None, None], jnp.exp(scores - row_max), 0.0)
    row_total = jnp.sum(exp_scores, axis=-1, keepdims=True)
    weights = (exp_scores / row_total).astype(jnp.bfloat16)
    attended = jnp.einsum("hgqk,khd->qhgd", weights, value_rows, preferred_element_type=jnp.float32)
    return jnp.sum(attended.reshape(row_count, -1) * folded_head[None, :], axis=1)


def local(
    hidden,
    rewards,
    lengths,
    dest_shard,
    source_owner,
    pack_offset,
    segment_ids,
    norm_gain,
    w_query,
    w_key,
    w_value,
    value_head,
    folded_head,
):
    shards = lax.axis_size("dp")
    shard_index = lax.axis_index("dp")
    rollouts = lengths.shape[0]
    slot_rows = rewards.shape[1]
    packed_rows = segment_ids.shape[0]
    part_width = hidden.shape[1]
    slot_lanes = jnp.arange(rollouts, dtype=jnp.int32)

    def slot_for(shift_by):
        target = (shard_index + shift_by) % shards
        return jnp.sum(jnp.where(dest_shard == target, slot_lanes, 0))

    def outgoing(shift_by, source):
        return lax.dynamic_slice_in_dim(source, slot_for(shift_by) * slot_rows, slot_rows, 0)

    source_step = (shard_index - source_owner) % shards
    lane_match = segment_ids[:, None] == slot_lanes[None, :]
    row_step = jnp.sum(jnp.where(lane_match, source_step[None, :], 0), axis=1)
    row_offset = jnp.sum(jnp.where(lane_match, pack_offset[None, :], 0), axis=1)
    positions = jnp.arange(packed_rows, dtype=jnp.int32) - row_offset
    pick_rows = row_step * slot_rows + positions
    full_rows = lax.all_gather(hidden, "mp", axis=1, tiled=True)
    received = [outgoing(0, full_rows)]
    for shift_by in range(1, rollouts):
        received.append(passed_along(outgoing(shift_by, full_rows), "dp", shift_by))
    packed = jnp.take(jnp.concatenate(received, axis=0), pick_rows, axis=0)
    packed_f = packed.astype(jnp.float32)
    row_scale = lax.rsqrt(jnp.mean(packed_f * packed_f, axis=1) + EPSILON)
    normed = (packed_f * row_scale[:, None] * norm_gain[None, :]).astype(jnp.bfloat16)
    queries = jnp.dot(normed, w_query, preferred_element_type=jnp.float32)
    keys_out = jnp.dot(normed, w_key, preferred_element_type=jnp.float32)
    values_out = jnp.dot(normed, w_value, preferred_element_type=jnp.float32)
    own_part = lax.dynamic_slice_in_dim(packed, lax.axis_index("mp") * part_width, part_width, 1)
    value_terms = head_values(queries, keys_out, values_out, segment_ids, positions, folded_head)
    value_terms = value_terms + jnp.sum(own_part.astype(jnp.float32) * value_head[None, :], axis=1)
    packed_values = lax.psum(value_terms, "mp")
    padded = jnp.concatenate([packed_values, jnp.zeros((slot_rows,), jnp.float32)])
    slot_values = jnp.zeros((rollouts, slot_rows), jnp.float32)
    for shift_by in range(rollouts):
        owner_now = (shard_index - shift_by) % shards
        j_index = jnp.sum(jnp.where(source_owner == owner_now, slot_lanes, 0))
        start_at = jnp.sum(jnp.where(slot_lanes == j_index, pack_offset, 0))
        arrived = lax.dynamic_slice_in_dim(padded, start_at, slot_rows, 0)
        if shift_by:
            arrived = passed_along(arrived, "dp", -shift_by)
        slot_values = jnp.where(
            (slot_lanes == slot_for(shift_by))[:, None], arrived[None, :], slot_values
        )
    step_ids = jnp.arange(slot_rows, dtype=jnp.int32)
    live_mask = step_ids[None, :] < lengths[:, None]
    values = jnp.where(live_mask, slot_values, 0.0)
    next_live = step_ids[None, :] + 1 < lengths[:, None]
    following = jnp.concatenate([values[:, 1:], jnp.zeros((rollouts, 1), jnp.float32)], axis=1)
    one_step = jnp.where(
        live_mask, rewards + DISCOUNT * jnp.where(next_live, following, 0.0) - values, 0.0
    )
    lag_matrix = (step_ids[:, None] - step_ids[None, :]).astype(jnp.float32)
    decay_table = jnp.where(
        lag_matrix >= 0, jnp.exp(lag_matrix * math.log(DISCOUNT * SMOOTHING)), 0.0
    )
    advantages = jnp.dot(one_step, decay_table, precision=lax.Precision.HIGHEST)
    return (values, advantages)


def solution(mesh):
    return jax.shard_map(
        local,
        mesh=mesh,
        in_specs=(
            P("dp", "mp"),
            P("dp", None),
            P("dp"),
            P("dp"),
            P("dp"),
            P("dp"),
            P("dp"),
            P(),
            P(None, "mp"),
            P(None, "mp"),
            P(None, "mp"),
            P("mp"),
            P("mp"),
        ),
        out_specs=(P("dp", None), P("dp", None)),
        check_vma=False,
    )
```

profile of v0, /device:TPU:0, one launch (start us, length us, event | category | flops | bytes accessed | tf_op | source)
XLA Modules:
  0.0 758.3 jit_solution(953144892588931112)
XLA Ops:
  7.2 0.7 all-gather.2.cloned.1.call-update
  8.1 1.7 fusion.49
  15.0 129.0 %all-gather.2.cloned.1.call-done = bf16[1280,8192]{1,0:T(8,128)(2,1)} async-done(((bf16[1280,2048]{1,0:T(8,128)(2,1)}), bf16[1280,8192]{1,0:T(8,128)(2,1)}) %all-gather.2.cloned.1.call-update) | async-done | bytes 20971536 | tf_op jit(solution)/shard_map/all_gather | solution.py:95
  143.9 14.7 %constant_dynamic-slice_fusion = (bf16[160,8192]{1,0:T(8,128)(2,1)}, bf16[160,8192]{1,0:T(8,128)(2,1)}, bf16[160,8192]{1,0:T(8,128)(2,1)}, bf16[160,8192]{1,0:T(...) fusion(bf16[1280,8192]{1,0:T(8,128)(2,1)} %all-gather.2.cloned., ...), kind=kLoop, calls=%fused_computation.95 | loop fusion | bytes 41943072 | tf_op jit(solution)/shard_map/dynamic_slice | solution.py:87
  158.7 1.5 collective-permute-start
  160.2 5.7 fusion.58
  181.0 0.7 iota_compare_fusion.10
  181.7 1.5 collective-permute-start.1
  183.2 0.7 iota_compare_fusion.3
  184.5 0.7 iota_compare_fusion.5
  185.2 0.6 iota_compare_fusion.6
  185.8 0.7 iota_compare_fusion.7
  186.5 2.5 collective-permute-start.2
  189.4 1.2 multiply_cosine_fusion
  190.6 1.5 collective-permute-start.3
  192.1 2.4 collective-permute-start.4
  194.5 27.1 %collective-permute-done = bf16[160,8192]{1,0:T(8,128)(2,1)} collective-permute-done((bf16[160,8192]{1,0:T(8,128)(2,1)}, bf16[160,8192]{1,0:T(8,128)(2,1)}, u32[]{:S(2)}, u32[]{:S(2)}) %collective-permute-start) | collective-permute-done | bytes 2621472 | tf_op jit(solution)/shard_map/ppermute | solution.py:19
  221.6 1.3 collective-permute-start.5
  223.0 3.5 constant_dynamic-update-slice_fusion.6
  226.5 17.2 %collective-permute-done.1 = bf16[160,8192]{1,0:T(8,128)(2,1)S(1)} collective-permute-done((bf16[160,8192]{1,0:T(8,128)(2,1)}, bf16[160,8192]{1,0:T(8,128)(2,1)S(1)}, u32[]{:S(2)}, u32[]{:S(2)}) %collective-permute-start.1) | collective-permute-done | bytes 2621472 | tf_op jit(solution)/shard_map/ppermute | solution.py:19
  243.7 34.9 %collective-permute-start.6 = (bf16[160,8192]{1,0:T(8,128)(2,1)}, bf16[160,8192]{1,0:T(8,128)(2,1)S(1)}, u32[]{:S(2)}, u32[]{:S(2)}) collective-permute-start(bf16[160,8192]{1,0:T(8,128)(2,1)} %get-tuple-element.30), channel_id=1, source_target_pairs={{0,28},{4,0},{8,4},{12,8},{16,12},{20,16},{24,20},{28,24},{1,29},{... | collective-permute-start | bytes 7864328 | tf_op jit(solution)/shard_map/ppermute | solution.py:19
  278.6 1.7 constant_dynamic-update-slice_fusion.5
  280.3 165.2 %collective-permute-done.2 = bf16[160,8192]{1,0:T(8,128)(2,1)S(1)} collective-permute-done((bf16[160,8192]{1,0:T(8,128)(2,1)}, bf16[160,8192]{1,0:T(8,128)(2,1)S(1)}, u32[]{:S(2)}, u32[]{:S(2)}) %collective-permute-start.2) | collective-permute-done | bytes 2621472 | tf_op jit(solution)/shard_map/ppermute | solution.py:19
  445.5 1.8 constant_dynamic-update-slice_fusion.4
  447.3 20.0 %collective-permute-done.3 = bf16[160,8192]{1,0:T(8,128)(2,1)S(1)} collective-permute-done((bf16[160,8192]{1,0:T(8,128)(2,1)}, bf16[160,8192]{1,0:T(8,128)(2,1)S(1)}, u32[]{:S(2)}, u32[]{:S(2)}) %collective-permute-start.3) | collective-permute-done | bytes 2621472 | tf_op jit(solution)/shard_map/ppermute | solution.py:19
  467.3 1.7 constant_dynamic-update-slice_fusion.3
  469.1 1.7 constant_dynamic-update-slice_fusion.2
  470.8 1.7 constant_dynamic-update-slice_fusion.1
  472.5 48.2 %collective-permute-done.6 = bf16[160,8192]{1,0:T(8,128)(2,1)S(1)} collective-permute-done((bf16[160,8192]{1,0:T(8,128)(2,1)}, bf16[160,8192]{1,0:T(8,128)(2,1)S(1)}, u32[]{:S(2)}, u32[]{:S(2)}) %collective-permute-start.6) | collective-permute-done | bytes 2621472 | tf_op jit(solution)/shard_map/ppermute | solution.py:19
  520.7 1.7 constant_dynamic-update-slice_fusion
  522.4 31.2 %gather_fusion = bf16[640,8192]{1,0:T(8,128)(2,1)} fusion(bf16[1280,8192]{1,0:T(8,128)(2,1)} %constant_dynamic-update-slice_fusion, s32[1024]{0:T(1024)S(1)} %pad_clamp_fusion), kind=kCustom, calls=%fused_computation | custom fusion | bytes 20974080 | tf_op jit(solution)/shard_map/jit(_take)/gather | solution.py:99
  553.6 7.7 %fusion = (f32[640]{0:T(1024)S(1)}, bf16[640,8192]{1,0:T(8,128)(2,1)S(1)}) fusion(bf16[640,8192]{1,0:T(8,128)(2,1)} %gather_fusion, pred[640]{0:T(1024)(128)(4,1)S(1)} %compare_and_fusion.1), kind=kLoop, calls=%fused_computation.3 | loop fusion | flops 20970880 | bytes 20974720 | tf_op jit(solution)/shard_map/reduce_sum | solution.py:101
  561.3 3.3 convolution_bitcast_fusion.1
  564.6 0.7 fusion.36
  565.3 14.4 %convolution_bitcast_fusion = f32[80,8,8,128]{3,1,2,0:T(8,128)S(1)} fusion(bf16[8192,1024]{1,0:T(8,128)(2,1)} %param.21, bf16[640,8192]{1,0:T(8,128)(2,1)S(1)} %get-tuple-element.29, f32[8192]{0:T(1024)S(1)} %copy-done.8, f32[640]{0:T(1024)S(1)} %add_rsqrt_fusion), kind=kOutput, calls=%fused_computation.20 | convolution fusion | flops 10758389760 | bytes 29919744 | tf_op jit(solution)/shard_map/dot_general | solution.py:103
  580.3 0.8 fusion.86
  581.2 1.0 subtract_convert_fusion
  582.2 6.4 fusion.3
  588.6 7.8 %fusion.4 = f32[8,640]{1,0:T(8,128)S(1)} fusion(f32[640,640,8]{1,0,2:T(8,128)} %get-tuple-element.58, f32[8,640]{1,0:T(8,128)S(1)} %get-tuple-element.57, pred[640,640]{0,1:T(8,128)(4,1)S(1)} %compare_and_fusion), kind=kLoop, calls=%fused_computation.11 | loop fusion | flops 16378880 | bytes 13557760 | tf_op jit(solution)/shard_map/reduce_sum | solution.py:53
  597.1 14.9 %fusion.7 = f32[640]{0:T(1024)S(1)} fusion(f32[8,640]{1,0:T(8,128)S(1)} %fusion.4, f32[8,640]{1,0:T(8,128)S(1)} %get-tuple-element.57, f32[640,640,8]{1,0,2:T(8,128)} %get-tuple-element.58, pred[640,640]{0,1:T(8,128)(4,1)S(1)} %compare_and_fusion, f32[8,128]{1,0:T(8,128)S(1)} %bitcast.51, bf16[8192,128]{1,0:T(8,128)(2,1)} %param.23, ...), kind=kOutput, calls=%fused_computation.16 | convolution fusion | flops 2223062528 | bytes 26182656 | tf_op jit(solution)/shard_map/hgqk,khd->qhgd/dot_general | solution.py:55
  612.0 6.0 psum.7
  618.1 114.7 %collective-permute-start.10 = (f32[160]{0:T(256)S(1)}, f32[160]{0:T(256)S(1)}, u32[]{:S(2)}, u32[]{:S(2)}) collective-permute-start(f32[160]{0:T(256)S(1)} %get-tuple-element.49), channel_id=1, source_target_pairs={{0,16},{4,20},{8,24},{12,28},{16,0},{20,4},{24,8},{28,12},{1,17},{... | collective-permute-start | bytes 1928 | tf_op jit(solution)/shard_map/ppermute | solution.py:19
  732.8 0.6 iota_compare_fusion.8
  733.4 9.1 %collective-permute-start.12 = (f32[160]{0:T(256)S(1)}, f32[160]{0:T(256)S(1)}, u32[]{:S(2)}, u32[]{:S(2)}) collective-permute-start(f32[160]{0:T(256)S(1)} %get-tuple-element.51), channel_id=1, source_target_pairs={{0,24},{4,28},{8,0},{12,4},{16,8},{20,12},{24,16},{28,20},{1,25},{... | collective-permute-start | bytes 1928 | tf_op jit(solution)/shard_map/ppermute | solution.py:19
  742.5 2.0 collective-permute-start.7
  746.1 2.7 collective-permute-done.7
  748.8 1.1 collective-permute-done.8
  750.1 0.8 fusion.25
  (52 shorter events, 4.3 us)
Async XLA Ops:
  7.2 554.1 %copy-start = (bf16[8192,128]{1,0:T(8,128)(2,1)S(1)}, bf16[8192,128]{1,0:T(8,128)(2,1)}, u32[]{:S(2)}) copy-start(bf16[8192,128]{1,0:T(8,128)(2,1)} %param.22) | copy-start | bytes 6291460
  7.2 136.8 %all-gather.2.cloned.1.call-start = ((), (), s32[]{:S(2)}) async-start(), calls=%async_computation | async-start | bytes 26214400 | tf_op jit(solution)/shard_map/all_gather | solution.py:95
  14.9 145.2 %copy-start.6 = (s32[8]{0:T(128)S(1)}, s32[8]{0:T(128)}, u32[]{:S(2)}) copy-start(s32[8]{0:T(128)} %param.18) | copy-start | bytes 100
  15.0 165.9 %copy-start.3 = (s32[640]{0:T(1024)S(1)}, s32[640]{0:T(1024)}, u32[]{:S(2)}) copy-start(s32[640]{0:T(1024)} %param.19) | copy-start | bytes 7684
  158.7 63.0 %collective-permute-start = (bf16[160,8192]{1,0:T(8,128)(2,1)}, bf16[160,8192]{1,0:T(8,128)(2,1)}, u32[]{:S(2)}, u32[]{:S(2)}) collective-permute-start(bf16[160,8192]{1,0:T(8,128)(2,1)} %get-tuple-element.36), channel_id=1, source_target_pairs={{0,4},{4,8},{8,12},{12,16},{16,20},{20,24},{24,28},{28,0},{1,5},{5... | collective-permute-start | bytes 7864328 | tf_op jit(solution)/shard_map/ppermute | solution.py:19
  181.7 62.0 %collective-permute-start.1 = (bf16[160,8192]{1,0:T(8,128)(2,1)}, bf16[160,8192]{1,0:T(8,128)(2,1)S(1)}, u32[]{:S(2)}, u32[]{:S(2)}) collective-permute-start(bf16[160,8192]{1,0:T(8,128)(2,1)} %get-tuple-element.35), channel_id=1, source_target_pairs={{0,8},{4,12},{8,16},{12,20},{16,24},{20,28},{24,0},{28,4},{1,9},{5... | collective-permute-start | bytes 7864328 | tf_op jit(solution)/shard_map/ppermute | solution.py:19
  186.5 259.0 %collective-permute-start.2 = (bf16[160,8192]{1,0:T(8,128)(2,1)}, bf16[160,8192]{1,0:T(8,128)(2,1)S(1)}, u32[]{:S(2)}, u32[]{:S(2)}) collective-permute-start(bf16[160,8192]{1,0:T(8,128)(2,1)} %get-tuple-element.34), channel_id=1, source_target_pairs={{0,12},{4,16},{8,20},{12,24},{16,28},{20,0},{24,4},{28,8},{1,13},{... | collective-permute-start | bytes 7864328 | tf_op jit(solution)/shard_map/ppermute | solution.py:19
  190.6 276.7 %collective-permute-start.3 = (bf16[160,8192]{1,0:T(8,128)(2,1)}, bf16[160,8192]{1,0:T(8,128)(2,1)S(1)}, u32[]{:S(2)}, u32[]{:S(2)}) collective-permute-start(bf16[160,8192]{1,0:T(8,128)(2,1)} %get-tuple-element.33), channel_id=1, source_target_pairs={{0,16},{4,20},{8,24},{12,28},{16,0},{20,4},{24,8},{28,12},{1,17},{... | collective-permute-start | bytes 7864328 | tf_op jit(solution)/shard_map/ppermute | solution.py:19
  192.1 277.0 %collective-permute-start.4 = (bf16[160,8192]{1,0:T(8,128)(2,1)}, bf16[160,8192]{1,0:T(8,128)(2,1)S(1)}, u32[]{:S(2)}, u32[]{:S(2)}) collective-permute-start(bf16[160,8192]{1,0:T(8,128)(2,1)} %get-tuple-element.32), channel_id=1, source_target_pairs={{0,20},{4,24},{8,28},{12,0},{16,4},{20,8},{24,12},{28,16},{1,21},{... | collective-permute-start | bytes 7864328 | tf_op jit(solution)/shard_map/ppermute | solution.py:19
  221.6 249.2 %collective-permute-start.5 = (bf16[160,8192]{1,0:T(8,128)(2,1)}, bf16[160,8192]{1,0:T(8,128)(2,1)S(1)}, u32[]{:S(2)}, u32[]{:S(2)}) collective-permute-start(bf16[160,8192]{1,0:T(8,128)(2,1)} %get-tuple-element.31), channel_id=1, source_target_pairs={{0,24},{4,28},{8,0},{12,4},{16,8},{20,12},{24,16},{28,20},{1,25},{... | collective-permute-start | bytes 7864328 | tf_op jit(solution)/shard_map/ppermute | solution.py:19
  243.7 277.1 %collective-permute-start.6 = (bf16[160,8192]{1,0:T(8,128)(2,1)}, bf16[160,8192]{1,0:T(8,128)(2,1)S(1)}, u32[]{:S(2)}, u32[]{:S(2)}) collective-permute-start(bf16[160,8192]{1,0:T(8,128)(2,1)} %get-tuple-element.30), channel_id=1, source_target_pairs={{0,28},{4,0},{8,4},{12,8},{16,12},{20,16},{24,20},{28,24},{1,29},{... | collective-permute-start | bytes 7864328 | tf_op jit(solution)/shard_map/ppermute | solution.py:19
  553.6 7.7 %copy-start.8 = (f32[8192]{0:T(1024)S(1)}, f32[8192]{0:T(1024)}, u32[]{:S(2)}) copy-start(f32[8192]{0:T(1024)} %param.20) | copy-start | bytes 98308
  561.3 35.2 %copy-start.2 = (bf16[640,8192]{1,0:T(8,128)(2,1)}, bf16[640,8192]{1,0:T(8,128)(2,1)S(1)}, u32[]{:S(2)}) copy-start(bf16[640,8192]{1,0:T(8,128)(2,1)S(1)} %get-tuple-element.29) | copy-start | bytes 31457284
  588.6 7.9 %copy-start.5 = (f32[2048]{0:T(1024)S(1)}, f32[2048]{0:T(1024)}, u32[]{:S(2)}) copy-start(f32[2048]{0:T(1024)} %param.24) | copy-start | bytes 24580
  588.6 8.5 %copy-start.10 = (f32[1024]{0:T(1024)S(1)}, f32[1024]{0:T(1024)}, u32[]{:S(2)}) copy-start(f32[1024]{0:T(1024)} %param.25) | copy-start | bytes 12292
  597.1 152.9 %copy-start.7 = (s32[8]{0:T(128)S(1)}, s32[8]{0:T(128)}, u32[]{:S(2)}) copy-start(s32[8]{0:T(128)} %param.15) | copy-start | bytes 100
  597.1 153.1 %copy-start.9 = (f32[8,160]{1,0:T(8,128)S(1)}, f32[8,160]{1,0:T(8,128)}, u32[]{:S(2)}) copy-start(f32[8,160]{1,0:T(8,128)} %param.14) | copy-start | bytes 15364
  597.1 153.9 %copy-start.1 = (bf16[8192,128]{1,0:T(8,128)(2,1)S(1)}, bf16[8192,128]{1,0:T(8,128)(2,1)}, u32[]{:S(2)}) copy-start(bf16[8192,128]{1,0:T(8,128)(2,1)} %param.22) | copy-start | bytes 6291460
  618.1 126.5 %collective-permute-start.10 = (f32[160]{0:T(256)S(1)}, f32[160]{0:T(256)S(1)}, u32[]{:S(2)}, u32[]{:S(2)}) collective-permute-start(f32[160]{0:T(256)S(1)} %get-tuple-element.49), channel_id=1, source_target_pairs={{0,16},{4,20},{8,24},{12,28},{16,0},{20,4},{24,8},{28,12},{1,17},{... | collective-permute-start | bytes 1928 | tf_op jit(solution)/shard_map/ppermute | solution.py:19
  732.8 11.8 %collective-permute-start.11 = (f32[160]{0:T(256)S(1)}, f32[160]{0:T(256)S(1)}, u32[]{:S(2)}, u32[]{:S(2)}) collective-permute-start(f32[160]{0:T(256)S(1)} %get-tuple-element.50), channel_id=1, source_target_pairs={{0,20},{4,24},{8,28},{12,0},{16,4},{20,8},{24,12},{28,16},{1,21},{... | collective-permute-start | bytes 1928 | tf_op jit(solution)/shard_map/ppermute | solution.py:19
  733.4 12.3 %collective-permute-start.12 = (f32[160]{0:T(256)S(1)}, f32[160]{0:T(256)S(1)}, u32[]{:S(2)}, u32[]{:S(2)}) collective-permute-start(f32[160]{0:T(256)S(1)} %get-tuple-element.51), channel_id=1, source_target_pairs={{0,24},{4,28},{8,0},{12,4},{16,8},{20,12},{24,16},{28,20},{1,25},{... | collective-permute-start | bytes 1928 | tf_op jit(solution)/shard_map/ppermute | solution.py:19
  742.5 3.6 collective-permute-start.13
  742.5 6.3 collective-permute-start.7
  744.5 5.4 collective-permute-start.8
  744.5 5.4 collective-permute-start.9
  750.0 0.9 copy-start.4
Sparse Core Ops, SparseCore 0:
  9.6 134.3 all-gather.1
where the time goes:
time: 765 us; the launch traced here: 758 us
  waiting for transfers between devices  412 us (54%)
  starting transfers between devices  172 us (22%)
  local copies, waits for them, and re-layouts  61.4 us (8%)
  matrix products  39.8 us (5%)
  between operations  35.1 us (5%)
  other arithmetic  32.1 us (4%)
    ppermute x14, waiting for transfers between devices, passed_along(): lax.ppermute(value, axis, [(i, (i + by) % length) for i in range(length)])  282 us
    ppermute x14, starting transfers between devices, passed_along(): lax.ppermute(value, axis, [(i, (i + by) % length) for i in range(length)])  172 us
    all_gather x1, waiting for transfers between devices, local(): full_rows = lax.all_gather(hidden, 'mp', axis=1, tiled=True)  129 us
    gather x1, local copies, waits for them, and re-layouts, local(): packed = jnp.take(jnp.concatenate(received, axis=0), pick_rows, axis=0)  31.2 us
  transfers between devices with their start and end apart: 15, of which 10 were waited for; matrix products, arithmetic and copies ran while one was open for 3% of the time, Pallas kernels for 0%

commit v1 on v0

v1 whole, which is shorter than its diff:
```python
import functools
import math

import jax
import jax.numpy as jnp
from jax import lax
from jax.experimental import pallas as pl
from jax.experimental.pallas import tpu as pltpu
from jax.sharding import PartitionSpec as P

HD = 128
EPSILON = 1e-05
DISCOUNT = 0.99
SMOOTHING = 0.95
ROPE_BASE = 500000.0
DEPTH = 1024


def swapped(value, axis, bit):
    length = lax.axis_size(axis)
    return lax.ppermute(value, axis, [(i, i ^ bit) for i in range(length)])


def lane_groups(value):
    total = value[:, :HD]
    for at in range(HD, value.shape[1], HD):
        total = total + value[:, at : at + HD]
    return total


def add_products(x, gain_ref, wq_ref, wk_ref, wv_ref, q_acc, kv_acc, ss_acc):
    xf = x.astype(jnp.float32)
    ss_acc[...] += lane_groups(xf * xf)
    scaled = (xf * gain_ref[...]).astype(jnp.bfloat16)
    q_acc[...] += jnp.dot(scaled, wq_ref[...], preferred_element_type=jnp.float32)
    kv_acc[:, :HD] += jnp.dot(scaled, wk_ref[...], preferred_element_type=jnp.float32)
    kv_acc[:, HD:] += jnp.dot(scaled, wv_ref[...], preferred_element_type=jnp.float32)


def first_kernel(
    part_ref, own_ref, near_ref, gain_ref, wq_ref, wk_ref, wv_ref, head_ref,
    q_ref, kv_ref, ss_ref, vt_ref,
):
    step = pl.program_id(0)
    half = pl.num_programs(0) // 2

    @pl.when(step == 0)
    def _():
        q_ref[...] = jnp.zeros_like(q_ref)
        kv_ref[...] = jnp.zeros_like(kv_ref)
        ss_ref[...] = jnp.zeros_like(ss_ref)
        vt_ref[...] = jnp.zeros_like(vt_ref)

    weights = (gain_ref, wq_ref, wk_ref, wv_ref)

    @pl.when(step < half)
    def _():
        vt_ref[...] += lane_groups(own_ref[...].astype(jnp.float32) * head_ref[...])
        add_products(own_ref[...], *weights, q_ref, kv_ref, ss_ref)

    @pl.when(step >= half)
    def _():
        add_products(near_ref[...], *weights, q_ref, kv_ref, ss_ref)


def second_kernel(
    slot, part_ref, x0_ref, x1_ref, gain_ref, wq_ref, wk_ref, wv_ref,
    q_ref, kv_ref, ss_ref, vt_ref, cos_ref, sin_ref, folded_ref,
    out_ref, q_acc, kv_acc, ss_acc,
):
    step = pl.program_id(0)
    steps = pl.num_programs(0)
    rows = q_acc.shape[0]
    heads = q_acc.shape[1] // HD

    @pl.when(step == 0)
    def _():
        q_acc[...] = q_ref[...]
        kv_acc[...] = kv_ref[...]
        ss_acc[...] = ss_ref[...]

    weights = (gain_ref, wq_ref, wk_ref, wv_ref)

    @pl.when(step < steps // 2)
    def _():
        add_products(x0_ref[...], *weights, q_acc, kv_acc, ss_acc)

    @pl.when(step >= steps // 2)
    def _():
        add_products(x1_ref[...], *weights, q_acc, kv_acc, ss_acc)

    @pl.when(step == steps - 1)
    def _():
        features = DEPTH * steps * 2
        cosine, sine = cos_ref[...], sin_ref[...]
        row_at = lax.broadcasted_iota(jnp.int32, (slot, slot), 0)
        key_at = lax.broadcasted_iota(jnp.int32, (slot, slot), 1)
        allowed = row_at >= key_at
        ones = jnp.ones((8, HD), jnp.float32)

        def turned(value):
            return (value * cosine + pltpu.roll(value, HD // 2, 1) * sine).astype(jnp.bfloat16)

        def one_rollout(r, carry):
            here = pl.ds(pl.multiple_of(r * slot, 16), slot)
            mean = jnp.sum(ss_acc[here, :], axis=1, keepdims=True) / features
            scale = lax.rsqrt(mean + EPSILON)
            key = turned(kv_acc[here, :HD] * scale)
            val = (kv_acc[here, HD:] * scale).astype(jnp.bfloat16)
            total = vt_ref[here, :]
            for h in range(heads):
                query = turned(q_acc[here, h * HD : (h + 1) * HD] * scale)
                scores = lax.dot_general(
                    query, key, (((1,), (1,)), ((), ())), preferred_element_type=jnp.float32
                ) * (1.0 / math.sqrt(HD))
                scores = jnp.where(allowed, scores, -1e30)
                exps = jnp.exp(scores - jnp.max(scores, axis=1, keepdims=True))
                probs = (exps / jnp.sum(exps, axis=1, keepdims=True)).astype(jnp.bfloat16)
                attended = jnp.dot(probs, val, preferred_element_type=jnp.float32)
                total = total + attended * folded_ref[h : h + 1, :]
            out_ref[r] = lax.dot_general(
                ones, total, (((1,), (1,)), ((), ())),
                precision=lax.Precision.HIGHEST, preferred_element_type=jnp.float32,
            )
            return carry

        lax.fori_loop(0, rows // slot, one_rollout, 0)


def weight_specs(first, second, blocks, widths):
    def row(step, part_ref):
        flip = jnp.where(step < blocks, first, second)
        return (part_ref[0] ^ flip) * blocks + step % blocks

    return [pl.BlockSpec((1, DEPTH), lambda k, p: (0, row(k, p)))] + [
        pl.BlockSpec((DEPTH, width), lambda k, p: (row(k, p), 0)) for width in widths
    ]


def x_specs(rows, blocks):
    return [
        pl.BlockSpec((rows, DEPTH), lambda k, p: (0, jnp.minimum(k, blocks - 1))),
        pl.BlockSpec((rows, DEPTH), lambda k, p: (0, jnp.maximum(k - blocks, 0))),
    ]


def cost(rows, depth, columns):
    return pl.CostEstimate(
        flops=2 * rows * depth * columns,
        bytes_accessed=2 * depth * (rows + columns) + 4 * rows * columns,
        transcendentals=0,
    )


def local(
    hidden,
    rewards,
    lengths,
    dest_shard,
    source_owner,
    pack_offset,
    segment_ids,
    norm_gain,
    w_query,
    w_key,
    w_value,
    value_head,
    folded_head,
):
    rollouts, slot = rewards.shape
    rows, part_width = hidden.shape
    blocks = part_width // DEPTH
    q_width, kv_width = w_query.shape[1], w_key.shape[1]
    widths = (q_width, kv_width, kv_width)
    columns = sum(widths)
    part = lax.axis_index("mp").astype(jnp.int32)[None]
    gain = norm_gain[None, :]
    weights = (w_query, w_key, w_value)

    positions = jnp.arange(slot, dtype=jnp.float32)
    half = HD // 2
    frequency = ROPE_BASE ** (-jnp.arange(half, dtype=jnp.float32) / half)
    angles = positions[:, None] * frequency[None, :]
    cosine = jnp.concatenate([jnp.cos(angles)] * 2, axis=1)
    sine = jnp.concatenate([-jnp.sin(angles), jnp.sin(angles)], axis=1)

    near = swapped(hidden, "mp", 1)
    sums = pl.pallas_call(
        first_kernel,
        grid_spec=pltpu.PrefetchScalarGridSpec(
            num_scalar_prefetch=1,
            grid=(2 * blocks,),
            in_specs=x_specs(rows, blocks)
            + weight_specs(0, 1, blocks, widths)
            + [pl.BlockSpec((1, DEPTH), lambda k, p: (0, jnp.minimum(k, blocks - 1)))],
            out_specs=[
                pl.BlockSpec((rows, width), lambda k, p: (0, 0))
                for width in (q_width, 2 * kv_width, HD, HD)
            ],
        ),
        out_shape=[
            jax.ShapeDtypeStruct((rows, width), jnp.float32)
            for width in (q_width, 2 * kv_width, HD, HD)
        ],
        compiler_params=pltpu.CompilerParams(vmem_limit_bytes=56 << 20),
        cost_estimate=cost(rows, 2 * part_width, columns),
        name="own_half",
    )(part, hidden, near, gain, *weights, value_head[None, :])

    def far_half(begin, count, far, far_near):
        at = begin // count
        return pl.pallas_call(
            functools.partial(second_kernel, slot),
            grid_spec=pltpu.PrefetchScalarGridSpec(
                num_scalar_prefetch=1,
                grid=(2 * blocks,),
                in_specs=x_specs(count, blocks)
                + weight_specs(2, 3, blocks, widths)
                + [
                    pl.BlockSpec((count, width), lambda k, p: (at, 0))
                    for width in (q_width, 2 * kv_width, HD, HD)
                ]
                + [pl.BlockSpec((slot, HD), lambda k, p: (0, 0))] * 2
                + [pl.BlockSpec((q_width // HD, HD), lambda k, p: (0, 0))],
                out_specs=pl.BlockSpec((count // slot, 8, slot), lambda k, p: (0, 0, 0)),
                scratch_shapes=[
                    pltpu.VMEM((count, q_width), jnp.float32),
                    pltpu.VMEM((count, 2 * kv_width), jnp.float32),
                    pltpu.VMEM((count, HD), jnp.float32),
                ],
            ),
            out_shape=jax.ShapeDtypeStruct((count // slot, 8, slot), jnp.float32),
            compiler_params=pltpu.CompilerParams(vmem_limit_bytes=56 << 20),
            cost_estimate=cost(count, 2 * part_width, columns),
            name="far_half",
        )(
            part, far, far_near, gain, *weights, *sums, cosine, sine,
            folded_head.reshape(q_width // HD, HD),
        )[:, 0, :]

    terms = []
    begin = 0
    after = sums[3]
    for count in (3, 3, 1, 1):
        size = count * slot
        far = swapped(hidden[begin : begin + size], "mp", 2)
        far, after = lax.optimization_barrier((far, after))
        far_near = swapped(far, "mp", 1)
        terms.append(far_half(begin, size, far, far_near))
        after = terms[-1]
        begin += size
    slot_values = lax.psum(jnp.concatenate(terms, axis=0), "mp")

    step_ids = jnp.arange(slot, dtype=jnp.int32)
    live_mask = step_ids[None, :] < lengths[:, None]
    values = jnp.where(live_mask, slot_values, 0.0)
    next_live = step_ids[None, :] + 1 < lengths[:, None]
    following = jnp.concatenate([values[:, 1:], jnp.zeros((rollouts, 1), jnp.float32)], axis=1)
    one_step = jnp.where(
        live_mask, rewards + DISCOUNT * jnp.where(next_live, following, 0.0) - values, 0.0
    )
    lag_matrix = (step_ids[:, None] - step_ids[None, :]).astype(jnp.float32)
    decay_table = jnp.where(
        lag_matrix >= 0, jnp.exp(lag_matrix * math.log(DISCOUNT * SMOOTHING)), 0.0
    )
    advantages = jnp.dot(one_step, decay_table, precision=lax.Precision.HIGHEST)
    return (values, advantages)


def solution(mesh):
    return jax.shard_map(
        local,
        mesh=mesh,
        in_specs=(
            P("dp", "mp"),
            P("dp", None),
            P("dp"),
            P("dp"),
            P("dp"),
            P("dp"),
            P("dp"),
            P(),
            P(None, "mp"),
            P(None, "mp"),
            P(None, "mp"),
            P("mp"),
            P("mp"),
        ),
        out_specs=(P("dp", None), P("dp", None)),
        check_vma=False,
    )
```

time: 765 us -> 161 us (0.21)
  waiting for transfers between devices: 412 us -> 44.8 us
  starting transfers between devices: 172 us -> 8.57 us
  Pallas kernels: 0 us -> 83 us
  local copies, waits for them, and re-layouts: 61.4 us -> 14.2 us
  matrix products: 39.8 us -> 0.84 us
  between operations: 35.1 us -> 0.7 us
  other arithmetic: 32.1 us -> 1.21 us
    ppermute x14 -> x9, waiting for transfers between devices: 282 us -> 44.8 us  [swapped(): return lax.ppermute(value, axis, [(i, i ^ bit) for i in range(length)])]
    ppermute x14 -> x9, starting transfers between devices: 172 us -> 8.57 us  [swapped(): return lax.ppermute(value, axis, [(i, i ^ bit) for i in range(length)])]
    all_gather x1 -> x0, waiting for transfers between devices: 129 us -> none  [local(): full_rows = lax.all_gather(hidden, 'mp', axis=1, tiled=True)]
    pallas_call x0 -> x5, Pallas kernels: none -> 83 us  [the longest x4 55.7 us: far_half(): pl.pallas_call(functools.partial(second_kernel, slot), grid_spec=pltpu.Pr...]
    dot_general x4 -> x0, matrix products: 39 us -> none  [the longest x1 14.9 us: head_values(): jnp.einsum('hgqk,khd->qhgd', weights, value_rows, preferred_element_type=...]
    gather x1 -> x0, local copies, waits for them, and re-layouts: 31.2 us -> none  [local(): packed = jnp.take(jnp.concatenate(received, axis=0), pick_rows, axis=0)]
    reduce_sum x6 -> x0, other arithmetic: 23.6 us -> none  [the longest x1 7.85 us: head_values(): row_total = jnp.sum(exp_scores, axis=-1, keepdims=True)]
    dynamic_slice x2 -> x0, local copies, waits for them, and re-layouts: 14.8 us -> none  [the longest x1 14.7 us: outgoing(): lax.dynamic_slice_in_dim(source, slot_for(shift_by) * slot_rows, slot_row...]
  transfers between devices with their start and end apart: 15 -> 9, of which waited for: 10 -> 7; matrix products, arithmetic and copies ran while one was open for 3% -> 6% of each run, Pallas kernels for 0% -> 46%
where the time goes in v1:
time: 161 us
  Pallas kernels  83 us (52%)
  waiting for transfers between devices  44.8 us (28%)
  local copies, waits for them, and re-layouts  14.2 us (9%)
  starting transfers between devices  8.57 us (5%)
  blocking collectives  7.25 us (5%)
    pallas_call x4, Pallas kernels, far_half(): pl.pallas_call(functools.partial(second_kernel, slot), grid_spec=pltpu.Pr...  55.7 us
    ppermute x9, waiting for transfers between devices, swapped(): return lax.ppermute(value, axis, [(i, i ^ bit) for i in range(length)])  44.8 us
    pallas_call x1, Pallas kernels, local(): pl.pallas_call(first_kernel, grid_spec=pltpu.PrefetchScalarGridSpec(num_s...  27.3 us
    ppermute x9, starting transfers between devices, swapped(): return lax.ppermute(value, axis, [(i, i ^ bit) for i in range(length)])  8.57 us
    psum x1, blocking collectives, local(): slot_values = lax.psum(jnp.concatenate(terms, axis=0), 'mp')  7.25 us
    slice x2, local copies, waits for them, and re-layouts, local(): far = swapped(hidden[begin:begin + size], 'mp', 2)  6.77 us
    unnamed x24, local copies, waits for them, and re-layouts  4.45 us
  transfers between devices with their start and end apart: 9, of which 7 were waited for; matrix products, arithmetic and copies ran while one was open for 6% of the time, Pallas kernels for 46%

profile of v1, /device:TPU:0, one launch (start us, length us, event | category | flops | bytes accessed | tf_op | source)
XLA Modules:
  0.0 160.5 jit_solution(13768110685233512836)
XLA Ops:
  0.6 0.5 collective-permute-start.1
  1.1 4.6 %fusion.28 = (bf16[480,2048]{1,0:T(8,128)(2,1)}, bf16[480,2048]{1,0:T(8,128)(2,1)}) fusion(bf16[1280,2048]{1,0:T(8,128)(2,1)} %own_ref.1), kind=kLoop, calls=%fused_computation.40 | loop fusion | bytes 7864320 | tf_op jit(solution)/shard_map/slice | solution.py:246
  5.8 2.5 %collective-permute-start = (bf16[480,2048]{1,0:T(8,128)(2,1)}, bf16[480,2048]{1,0:T(8,128)(2,1)S(1)}, u32[]{:S(2)}, u32[]{:S(2)}) collective-permute-start(bf16[480,2048]{1,0:T(8,128)(2,1)} %get-tuple-element.18), channel_id=1, source_target_pairs={{0,2},{1,3},{2,0},{3,1},{4,6},{5,7},{6,4},{7,5},{8,10},{9,11},{10,... | collective-permute-start | bytes 5898248 | tf_op jit(solution)/shard_map/ppermute | solution.py:21
  8.3 1.5 collective-permute-done.1.near_ref
  9.8 27.3 %own_half.1 = (f32[1280,1024]{1,0:T(8,128)}, f32[1280,256]{1,0:T(8,128)}, f32[1280,128]{1,0:T(8,128)}, f32[1280,128]{1,0:T(8,128)}) custom-call(s32[1]{0:T(128)} %bitcast.part_ref, bf16[1280,2048]{1,0:T(8,128)(2,1)} %own_ref.1, bf16[1280,2048]{1,0:T(8,128)(2,1)} %collective-permute-done.1.near_ref, f32[1,8192]{1,0:T(1,128)} %bitcast.14, ...), custom_call_target="tpu_custom_call" | custom-call | flops 13421772800 | bytes 27525120 | tf_op jit(solution)/shard_map/own_half/pallas_call | solution.py:188
  37.0 15.0 %collective-permute-done.x0_ref = bf16[480,2048]{1,0:T(8,128)(2,1)S(1)} collective-permute-done((bf16[480,2048]{1,0:T(8,128)(2,1)}, bf16[480,2048]{1,0:T(8,128)(2,1)S(1)}, u32[]{:S(2)}, u32[]{:S(2)}) %collective-permute-start) | collective-permute-done | bytes 1966112 | tf_op jit(solution)/shard_map/ppermute | solution.py:21
  52.0 0.0 collective-permute-start.2
  52.0 1.7 %collective-permute-start.3 = (bf16[480,2048]{1,0:T(8,128)(2,1)}, bf16[480,2048]{1,0:T(8,128)(2,1)S(1)}, u32[]{:S(2)}, u32[]{:S(2)}) collective-permute-start(bf16[480,2048]{1,0:T(8,128)(2,1)} %get-tuple-element.19), channel_id=1, source_target_pairs={{0,2},{1,3},{2,0},{3,1},{4,6},{5,7},{6,4},{7,5},{8,10},{9,11},{10,... | collective-permute-start | bytes 5898248 | tf_op jit(solution)/shard_map/ppermute | solution.py:21
  53.8 0.3 fusion.12
  54.1 0.8 pad_maximum_fusion
  54.9 1.1 collective-permute-done.2.x1_ref
  56.0 0.0 copy-done
  56.0 1.3 copy-done.2
  57.3 18.1 %far_half.4 = f32[3,8,160]{2,1,0:T(8,128)} custom-call(s32[1]{0:T(128)} %bitcast.part_ref, bf16[480,2048]{1,0:T(8,128)(2,1)} %copy-done, bf16[480,2048]{1,0:T(8,128)(2,1)} %copy-done.2, f32[1,8192]{1,0:T(1,128)} %bitcast.15, bf16[8192,1024]{1,0:T(8,128)(2,1)} %wq_ref.9, bf16[8192,128]{1,0:T(8,128)(2,1)} %wk_ref.9, bf16[8192,128]{1,0:T(8,128)(2,1)} %wv_ref.9, ...), custom_call_target="tpu_custom_call" | custom-call | flops 5033164800 | bytes 16875520 | tf_op jit(solution)/shard_map/far_half/pallas_call | solution.py:212
  75.4 0.7 slice.36
  76.2 21.3 %collective-permute-done.3.x0_ref = bf16[480,2048]{1,0:T(8,128)(2,1)S(1)} collective-permute-done((bf16[480,2048]{1,0:T(8,128)(2,1)}, bf16[480,2048]{1,0:T(8,128)(2,1)S(1)}, u32[]{:S(2)}, u32[]{:S(2)}) %collective-permute-start.3) | collective-permute-done | bytes 1966112 | tf_op jit(solution)/shard_map/ppermute | solution.py:21
  97.5 0.0 collective-permute-start.4
  97.5 2.1 %fusion.29 = (bf16[160,2048]{1,0:T(8,128)(2,1)S(1)}, bf16[160,2048]{1,0:T(8,128)(2,1)S(1)}) fusion(bf16[1280,2048]{1,0:T(8,128)(2,1)} %own_ref.1), kind=kLoop, calls=%fused_computation.41 | loop fusion | bytes 2621440 | tf_op jit(solution)/shard_map/slice | solution.py:246
  99.6 1.8 %collective-permute-start.5 = (bf16[160,2048]{1,0:T(8,128)(2,1)S(1)}, bf16[160,2048]{1,0:T(8,128)(2,1)S(1)}, u32[]{:S(2)}, u32[]{:S(2)}) collective-permute-start(bf16[160,2048]{1,0:T(8,128)(2,1)S(1)} %get-tuple-element.20), channel_id=1, source_target_pairs={{0,2},{1,3},{2,0},{3,1},{4,6},{5,7},{6,4},{7,5},{8,10},{9,11},{10,... | collective-permute-start | bytes 1966088 | tf_op jit(solution)/shard_map/ppermute | solution.py:21
  101.4 0.0 collective-permute-done.4.x1_ref
  101.4 0.0 copy-done.1
  101.4 1.3 copy-done.3
  102.8 18.1 %far_half.5 = f32[3,8,160]{2,1,0:T(8,128)} custom-call(s32[1]{0:T(128)} %bitcast.part_ref, bf16[480,2048]{1,0:T(8,128)(2,1)} %copy-done.1, bf16[480,2048]{1,0:T(8,128)(2,1)} %copy-done.3, f32[1,8192]{1,0:T(1,128)} %bitcast.16, bf16[8192,1024]{1,0:T(8,128)(2,1)} %wq_ref.9, bf16[8192,128]{1,0:T(8,128)(2,1)} %wk_ref.9, bf16[8192,128]{1,0:T(8,128)(2,1)} %wv_ref.9, ...), custom_call_target="tpu_custom_call" | custom-call | flops 5033164800 | bytes 16875520 | tf_op jit(solution)/shard_map/far_half/pallas_call | solution.py:212
  120.9 0.7 slice.37
  121.6 0.0 collective-permute-done.5.x0_ref
  121.6 0.2 collective-permute-start.6
  121.8 1.8 %collective-permute-start.7 = (bf16[160,2048]{1,0:T(8,128)(2,1)S(1)}, bf16[160,2048]{1,0:T(8,128)(2,1)S(1)}, u32[]{:S(2)}, u32[]{:S(2)}) collective-permute-start(bf16[160,2048]{1,0:T(8,128)(2,1)S(1)} %get-tuple-element.21), channel_id=1, source_target_pairs={{0,2},{1,3},{2,0},{3,1},{4,6},{5,7},{6,4},{7,5},{8,10},{9,11},{10,... | collective-permute-start | bytes 1966088 | tf_op jit(solution)/shard_map/ppermute | solution.py:21
  123.6 0.2 collective-permute-done.6.x1_ref
  123.8 0.0 copy-done.5
  123.8 0.9 copy-done.7
  124.6 9.8 %far_half.6 = f32[1,8,160]{2,1,0:T(8,128)} custom-call(s32[1]{0:T(128)} %bitcast.part_ref, bf16[160,2048]{1,0:T(8,128)(2,1)} %copy-done.5, bf16[160,2048]{1,0:T(8,128)(2,1)} %copy-done.7, f32[1,8192]{1,0:T(1,128)} %bitcast.17, bf16[8192,1024]{1,0:T(8,128)(2,1)} %wq_ref.9, bf16[8192,128]{1,0:T(8,128)(2,1)} %wk_ref.9, bf16[8192,128]{1,0:T(8,128)(2,1)} %wv_ref.9, ...), custom_call_target="tpu_custom_call" | custom-call | flops 1677721600 | bytes 12615680 | tf_op jit(solution)/shard_map/far_half/pallas_call | solution.py:212
  134.4 0.7 slice_bitcast_fusion.1
  135.1 3.7 %collective-permute-done.7.x0_ref = bf16[160,2048]{1,0:T(8,128)(2,1)S(1)} collective-permute-done((bf16[160,2048]{1,0:T(8,128)(2,1)S(1)}, bf16[160,2048]{1,0:T(8,128)(2,1)S(1)}, u32[]{:S(2)}, u32[]{:S(2)}) %collective-permute-start.7) | collective-permute-done | bytes 655392 | tf_op jit(solution)/shard_map/ppermute | solution.py:21
  138.8 0.0 collective-permute-start.8
  138.8 0.0 copy-start.9
  138.9 0.0 copy-start.10
  138.9 2.1 %collective-permute-done.8.x1_ref = bf16[160,2048]{1,0:T(8,128)(2,1)S(1)} collective-permute-done((bf16[160,2048]{1,0:T(8,128)(2,1)S(1)}, bf16[160,2048]{1,0:T(8,128)(2,1)S(1)}, u32[]{:S(2)}, u32[]{:S(2)}) %collective-permute-start.8) | collective-permute-done | bytes 655392 | tf_op jit(solution)/shard_map/ppermute | solution.py:21
  140.9 0.0 copy-done.4
  140.9 0.9 copy-done.6
  141.8 9.8 %far_half.7 = f32[1,8,160]{2,1,0:T(8,128)} custom-call(s32[1]{0:T(128)} %bitcast.part_ref, bf16[160,2048]{1,0:T(8,128)(2,1)} %copy-done.4, bf16[160,2048]{1,0:T(8,128)(2,1)} %copy-done.6, f32[1,8192]{1,0:T(1,128)} %bitcast.18, bf16[8192,1024]{1,0:T(8,128)(2,1)} %wq_ref.9, bf16[8192,128]{1,0:T(8,128)(2,1)} %wk_ref.9, bf16[8192,128]{1,0:T(8,128)(2,1)} %wv_ref.9, ...), custom_call_target="tpu_custom_call" | custom-call | flops 1677721600 | bytes 12615680 | tf_op jit(solution)/shard_map/far_half/pallas_call | solution.py:212
  151.6 0.7 slice_bitcast_fusion
  152.3 7.3 %psum.7 = f32[8,160]{1,0:T(8,128)S(1)} all-reduce(f32[8,160]{1,0:T(8,128)S(1)} %pad_maximum_fusion.2), channel_id=1, replica_groups=mesh['dp'=8,'mp'=4] {'mp'}, use_global_device_ids=true, to_apply=%region_0.0 | all-reduce | flops 1280 | bytes 10240 | tf_op jit(solution)/shard_map/psum | solution.py:252
  159.5 0.0 copy-done.9
  159.5 0.1 fusion.19
  159.6 0.1 slice.40
  159.7 0.0 copy-done.10
  159.7 0.8 fusion
  160.5 0.0 copy-done.8
  (14 shorter events, 0.0 us)
Async XLA Ops:
  0.6 9.1 %collective-permute-start.1 = (bf16[1280,2048]{1,0:T(8,128)(2,1)}, bf16[1280,2048]{1,0:T(8,128)(2,1)}, u32[]{:S(2)}, u32[]{:S(2)}) collective-permute-start(bf16[1280,2048]{1,0:T(8,128)(2,1)} %own_ref.1), channel_id=1, source_target_pairs={{0,1},{1,0},{2,3},{3,2},{4,5},{5,4},{6,7},{7,6},{8,9},{9,8},{10,11... | collective-permute-start | bytes 15728648 | tf_op jit(solution)/shard_map/ppermute | solution.py:21
  5.8 46.2 %collective-permute-start = (bf16[480,2048]{1,0:T(8,128)(2,1)}, bf16[480,2048]{1,0:T(8,128)(2,1)S(1)}, u32[]{:S(2)}, u32[]{:S(2)}) collective-permute-start(bf16[480,2048]{1,0:T(8,128)(2,1)} %get-tuple-element.18), channel_id=1, source_target_pairs={{0,2},{1,3},{2,0},{3,1},{4,6},{5,7},{6,4},{7,5},{8,10},{9,11},{10,... | collective-permute-start | bytes 5898248 | tf_op jit(solution)/shard_map/ppermute | solution.py:21
  52.0 4.0 %copy-start = (bf16[480,2048]{1,0:T(8,128)(2,1)}, bf16[480,2048]{1,0:T(8,128)(2,1)S(1)}, u32[]{:S(2)}) copy-start(bf16[480,2048]{1,0:T(8,128)(2,1)S(1)} %collective-permute-done.x0_ref) | copy-start | bytes 5898244
  52.0 4.0 %collective-permute-start.2 = (bf16[480,2048]{1,0:T(8,128)(2,1)S(1)}, bf16[480,2048]{1,0:T(8,128)(2,1)S(1)}, u32[]{:S(2)}, u32[]{:S(2)}) collective-permute-start(bf16[480,2048]{1,0:T(8,128)(2,1)S(1)} %collective-permute-done.x0_ref), channel_id=1, source_target_pairs={{0,1},{1,0},{2,3},{3,2},{4,5},{5,4},{6,7},{7,6},{8,9},{9,8},{10,11... | collective-permute-start | bytes 5898248 | tf_op jit(solution)/shard_map/ppermute | solution.py:21
  52.0 45.4 %collective-permute-start.3 = (bf16[480,2048]{1,0:T(8,128)(2,1)}, bf16[480,2048]{1,0:T(8,128)(2,1)S(1)}, u32[]{:S(2)}, u32[]{:S(2)}) collective-permute-start(bf16[480,2048]{1,0:T(8,128)(2,1)} %get-tuple-element.19), channel_id=1, source_target_pairs={{0,2},{1,3},{2,0},{3,1},{4,6},{5,7},{6,4},{7,5},{8,10},{9,11},{10,... | collective-permute-start | bytes 5898248 | tf_op jit(solution)/shard_map/ppermute | solution.py:21
  56.0 1.3 copy-start.2
  97.5 4.0 %copy-start.1 = (bf16[480,2048]{1,0:T(8,128)(2,1)}, bf16[480,2048]{1,0:T(8,128)(2,1)S(1)}, u32[]{:S(2)}) copy-start(bf16[480,2048]{1,0:T(8,128)(2,1)S(1)} %collective-permute-done.3.x0_ref) | copy-start | bytes 5898244
  97.5 4.0 %collective-permute-start.4 = (bf16[480,2048]{1,0:T(8,128)(2,1)S(1)}, bf16[480,2048]{1,0:T(8,128)(2,1)S(1)}, u32[]{:S(2)}, u32[]{:S(2)}) collective-permute-start(bf16[480,2048]{1,0:T(8,128)(2,1)S(1)} %collective-permute-done.3.x0_ref), channel_id=1, source_target_pairs={{0,1},{1,0},{2,3},{3,2},{4,5},{5,4},{6,7},{7,6},{8,9},{9,8},{10,11... | collective-permute-start | bytes 5898248 | tf_op jit(solution)/shard_map/ppermute | solution.py:21
  99.6 22.0 %collective-permute-start.5 = (bf16[160,2048]{1,0:T(8,128)(2,1)S(1)}, bf16[160,2048]{1,0:T(8,128)(2,1)S(1)}, u32[]{:S(2)}, u32[]{:S(2)}) collective-permute-start(bf16[160,2048]{1,0:T(8,128)(2,1)S(1)} %get-tuple-element.20), channel_id=1, source_target_pairs={{0,2},{1,3},{2,0},{3,1},{4,6},{5,7},{6,4},{7,5},{8,10},{9,11},{10,... | collective-permute-start | bytes 1966088 | tf_op jit(solution)/shard_map/ppermute | solution.py:21
  101.4 1.3 copy-start.3
  121.6 2.2 %copy-start.5 = (bf16[160,2048]{1,0:T(8,128)(2,1)}, bf16[160,2048]{1,0:T(8,128)(2,1)S(1)}, u32[]{:S(2)}) copy-start(bf16[160,2048]{1,0:T(8,128)(2,1)S(1)} %collective-permute-done.5.x0_ref) | copy-start | bytes 1966084
  121.6 2.2 %collective-permute-start.6 = (bf16[160,2048]{1,0:T(8,128)(2,1)S(1)}, bf16[160,2048]{1,0:T(8,128)(2,1)S(1)}, u32[]{:S(2)}, u32[]{:S(2)}) collective-permute-start(bf16[160,2048]{1,0:T(8,128)(2,1)S(1)} %collective-permute-done.5.x0_ref), channel_id=1, source_target_pairs={{0,1},{1,0},{2,3},{3,2},{4,5},{5,4},{6,7},{7,6},{8,9},{9,8},{10,11... | collective-permute-start | bytes 1966088 | tf_op jit(solution)/shard_map/ppermute | solution.py:21
  121.8 17.0 %collective-permute-start.7 = (bf16[160,2048]{1,0:T(8,128)(2,1)S(1)}, bf16[160,2048]{1,0:T(8,128)(2,1)S(1)}, u32[]{:S(2)}, u32[]{:S(2)}) collective-permute-start(bf16[160,2048]{1,0:T(8,128)(2,1)S(1)} %get-tuple-element.21), channel_id=1, source_target_pairs={{0,2},{1,3},{2,0},{3,1},{4,6},{5,7},{6,4},{7,5},{8,10},{9,11},{10,... | collective-permute-start | bytes 1966088 | tf_op jit(solution)/shard_map/ppermute | solution.py:21
  123.8 0.9 copy-start.7
  138.8 2.1 %copy-start.4 = (bf16[160,2048]{1,0:T(8,128)(2,1)}, bf16[160,2048]{1,0:T(8,128)(2,1)S(1)}, u32[]{:S(2)}) copy-start(bf16[160,2048]{1,0:T(8,128)(2,1)S(1)} %collective-permute-done.7.x0_ref) | copy-start | bytes 1966084
  138.8 2.1 %collective-permute-start.8 = (bf16[160,2048]{1,0:T(8,128)(2,1)S(1)}, bf16[160,2048]{1,0:T(8,128)(2,1)S(1)}, u32[]{:S(2)}, u32[]{:S(2)}) collective-permute-start(bf16[160,2048]{1,0:T(8,128)(2,1)S(1)} %collective-permute-done.7.x0_ref), channel_id=1, source_target_pairs={{0,1},{1,0},{2,3},{3,2},{4,5},{5,4},{6,7},{7,6},{8,9},{9,8},{10,11... | collective-permute-start | bytes 1966088 | tf_op jit(solution)/shard_map/ppermute | solution.py:21
  138.8 20.7 %copy-start.9 = (s32[8]{0:T(128)S(1)}, s32[8]{0:T(128)}, u32[]{:S(2)}) copy-start(s32[8]{0:T(128)} %param.15) | copy-start | bytes 100
  138.9 20.8 %copy-start.10 = (f32[8,160]{1,0:T(8,128)S(1)}, f32[8,160]{1,0:T(8,128)}, u32[]{:S(2)}) copy-start(f32[8,160]{1,0:T(8,128)} %param.14) | copy-start | bytes 15364
  140.9 0.9 copy-start.6
  159.6 0.9 copy-start.8
